TPU v7x, 32 devices: a whole 2x2x4 slice. The times are simulated.
32 devices in a mesh: samp: 4 (over z), feat: 8 (over y, x, core).
Axes of the slice: x: 2, y: 2, z: 4, core: 2. Of those that a mesh axis runs over, the one named last changes fastest.
Arguments:
- design: bfloat16 [6144, 8192], P('samp', 'feat'), may hold values from -6 to 6
- labels: int32 [6144], P('samp'), may hold values 0 or 1
- coef_all: float32 [1048576], replicated, may hold values from -0.13 to 0.13
- active: int32 [8192], P('feat'), may hold values from 0 to 1048575, as said below
- penalty: float32 [8192], P('feat'), may hold values from 4 to 40
Outputs:
- gram: float32 [8192, 8192], P('samp', 'feat')
- gradient: float32 [8192], P('feat')
Inputs may be any that keep to these rules, and one draw needn't show every extreme that they name: `active`: the indices are distinct.
All inputs are finite; a program needn't handle non-finite values. No bound on the sum of `labels` on one device may be relied on, other than what follows from the above.
Results may differ from a plain program's by a relative error of at most 0.003.
Values may be sent and summed in bfloat16 or wider, within the bound.
A program may use at most 128 MiB of HBM per device.

v0:
```python
import jax
import jax.numpy as jnp
from jax import lax
from jax.sharding import PartitionSpec as P


def per_device(design, labels, coef_all, active, penalty):
    rows = design.shape[0]
    total_rows = rows * lax.axis_size("samp")
    scale = 1.0 / jnp.sqrt(jnp.float32(total_rows))
    beta = coef_all[active]
    partial_margin = jnp.dot(design, beta.astype(jnp.bfloat16), preferred_element_type=jnp.float32)
    margin = lax.psum(partial_margin, "feat")
    prob = 1.0 / (1.0 + jnp.exp(-margin))
    weight = prob * (1.0 - prob)
    resid = prob - labels.astype(jnp.float32)
    weighted = (design.astype(jnp.float32) * weight[:, None]).astype(jnp.bfloat16)
    resid_b = resid.astype(jnp.bfloat16)
    grad_part = jnp.dot(resid_b, design, preferred_element_type=jnp.float32)
    gradient = lax.psum(grad_part, "samp") * scale + penalty * beta
    terms = lax.dot_general(
        lax.all_gather(design, "feat", axis=1, tiled=True),
        weighted,
        (((0,), (0,)), ((), ())),
        preferred_element_type=jnp.float32,
    )
    gram = lax.psum_scatter(terms, "samp", scatter_dimension=0, tiled=True) * scale
    return (gram, gradient)


def solution(mesh):
    in_specs = (P("samp", "feat"), P("samp"), P(), P("feat"), P("feat"))
    out_specs = (P("samp", "feat"), P("feat"))
    return jax.shard_map(
        per_device, mesh=mesh, in_specs=in_specs, out_specs=out_specs, check_vma=False
    )
```

profile of v0, /device:TPU:28, one launch (start us, length us, event | category | flops | bytes accessed | tf_op | source)
XLA Modules:
  0.0 746.6 jit_solution(14373303194377786086)
XLA Ops:
  7.2 0.0 copy-start
  7.2 0.0 copy-start.1
  7.2 0.0 all-gather.2.cloned.1.call-start
  7.2 0.7 all-gather.2.cloned.1.call-update
  7.9 0.0 reduce-scatter.2.cloned.1.call-start
  8.0 0.9 fusion.1
  8.8 14.5 %gather_fusion = f32[1024]{0:T(1024)S(1)} fusion(f32[1048576]{0:T(1024)} %param.7, s32[1024]{0:T(1024)S(1)} %fusion.1), kind=kCustom, calls=%fused_computation | custom fusion | bytes 12288 | tf_op jit(solution)/shard_map/gather | solution.py:11
  23.3 0.0 copy-done
  23.3 0.9 convolution_reduce_fusion
  24.3 13.7 %psum.14 = f32[1536]{0:T(1024)S(1)} all-reduce(f32[1536]{0:T(1024)S(1)} %convolution_reduce_fusion), channel_id=1, replica_groups=mesh['samp'=4,'feat'=8] {'feat'}, use_global_device_ids=true, to_apply=%region_0.0 | all-reduce | flops 1536 | bytes 12288 | tf_op jit(solution)/shard_map/psum | solution.py:13
  38.0 0.0 copy-done.1
  38.0 97.5 %all-gather.2.cloned.1.call-done = bf16[1536,8192]{1,0:T(8,128)(2,1)} async-done(((bf16[1536,1024]{1,0:T(8,128)(2,1)}), bf16[1536,8192]{1,0:T(8,128)(2,1)}) %all-gather.2.cloned.1.call-update) | async-done | bytes 25165840 | tf_op jit(solution)/shard_map/all_gather | solution.py:22
  135.6 33.6 %convolution_bitcast_fusion = f32[8192,1024]{0,1:T(8,128)} fusion(bf16[1536,8192]{1,0:T(8,128)(2,1)} %all-gather.2.cloned.1.call-done, bf16[1536,1024]{1,0:T(8,128)(2,1)S(1)} %copy-done, f32[1536]{0:T(1024)S(1)} %get-tuple-element.7), kind=kOutput, calls=%fused_computation.1 | convolution fusion | flops 25774522368 | bytes 61872128 | tf_op jit(solution)/shard_map/dot_general | solution.py:21
  169.2 0.0 copy-start.2
  169.2 0.0 reduce-scatter.2.cloned.1.call-update
  169.2 0.5 fusion.2
  169.7 8.1 %psum.15 = f32[1024]{0:T(1024)S(1)} all-reduce(f32[1024]{0:T(1024)S(1)} %bitcast.8), channel_id=1, replica_groups=mesh['samp'=4,'feat'=8] {'samp'}, use_global_device_ids=true, to_apply=%region_2.0 | all-reduce | flops 1024 | bytes 8192 | tf_op jit(solution)/shard_map/psum | solution.py:20
  177.8 0.0 copy-done.2
  177.8 0.6 multiply_add_fusion
  178.4 543.7 %reduce-scatter.2.cloned.1.call-done = f32[2048,1024]{0,1:T(8,128)} async-done(((f32[8192,1024]{0,1:T(8,128)}), f32[2048,1024]{0,1:T(8,128)}) %reduce-scatter.2.cloned.1.call-update) | async-done | bytes 8388624 | tf_op jit(solution)/shard_map/reduce_scatter | solution.py:27
  722.1 8.4 %broadcast_multiply_fusion = f32[2048,1024]{0,1:T(8,128)} fusion(f32[2048,1024]{0,1:T(8,128)} %reduce-scatter.2.cloned.1.call-done), kind=kLoop, calls=%fused_computation.3 | loop fusion | flops 2097152 | bytes 16777216 | tf_op jit(solution)/shard_map/mul | solution.py:27
  730.5 9.2 %copy.8 = f32[2048,1024]{1,0:T(8,128)} copy(f32[2048,1024]{0,1:T(8,128)} %broadcast_multiply_fusion) | data formatting | bytes 16777216
  (4 shorter events, 0.0 us)
Async XLA Ops:
  7.2 16.2 %copy-start = (bf16[1536,1024]{1,0:T(8,128)(2,1)S(1)}, bf16[1536,1024]{1,0:T(8,128)(2,1)}, u32[]{:S(2)}) copy-start(bf16[1536,1024]{1,0:T(8,128)(2,1)} %param.5) | copy-start | bytes 9437188
  7.2 30.8 %copy-start.1 = (s32[1536]{0:T(1024)S(1)}, s32[1536]{0:T(1024)}, u32[]{:S(2)}) copy-start(s32[1536]{0:T(1024)} %param.6) | copy-start | bytes 18436
  7.2 128.4 %all-gather.2.cloned.1.call-start = ((), (), s32[]{:S(2)}) async-start(), calls=%async_computation.1 | async-start | bytes 28311552 | tf_op jit(solution)/shard_map/all_gather | solution.py:22
  7.9 714.1 %reduce-scatter.2.cloned.1.call-start = ((), (), s32[]{:S(2)}) async-start(), calls=%async_computation.2 | async-start | bytes 41943040 | tf_op jit(solution)/shard_map/reduce_scatter | solution.py:27
  169.2 8.6 %copy-start.2 = (f32[1024]{0:T(1024)S(1)}, f32[1024]{0:T(1024)}, u32[]{:S(2)}) copy-start(f32[1024]{0:T(1024)} %param.9) | copy-start | bytes 12292
Sparse Core Ops, SparseCore 0:
  9.9 125.5 all-gather.1
  169.3 552.7 reduce-scatter.1
where the time goes:
time: 749 us; the launch traced here: 747 us
  waiting for transfers between devices  642 us (86%)
  matrix products  35 us (5%)
  local copies, waits for them, and re-layouts  23.8 us (3%)
  blocking collectives  21.8 us (3%)
  between operations  14.1 us (2%)
  other arithmetic  9.89 us (1%)
    reduce_scatter x1, waiting for transfers between devices, per_device(): lax.psum_scatter(terms, 'samp', scatter_dimension=0, tiled=True) * scale  544 us
    all_gather x1, waiting for transfers between devices, per_device(): lax.all_gather(design, 'feat', axis=1, tiled=True)  97.5 us
    dot_general x1, matrix products, per_device(): lax.dot_general(lax.all_gather(design, 'feat', axis=1, tiled=True), weigh...  33.6 us
  transfers between devices with their start and end apart: 2, of which 2 were waited for; matrix products, arithmetic and copies ran while one was open for 2% of the time, Pallas kernels for 0%

commit v1 on v0

--- a/solution.py
+++ b/solution.py
@@ -24,7 +24,7 @@
         (((0,), (0,)), ((), ())),
         preferred_element_type=jnp.float32,
     )
-    gram = lax.psum_scatter(terms, "samp", scatter_dimension=0, tiled=True) * scale
+    gram = lax.psum_scatter(terms.astype(jnp.bfloat16), "samp", scatter_dimension=0, tiled=True).astype(jnp.float32) * scale
     return (gram, gradient)
 
 

time: 749 us -> 475 us (0.63)
  waiting for transfers between devices: 642 us -> 370 us
    reduce_scatter x1, waiting for transfers between devices: 544 us -> 272 us  [per_device(): lax.psum_scatter(terms.astype(jnp.bfloat16), 'samp', scatter_dimension=0,...]
  transfers between devices with their start and end apart: 2 -> 2, of which waited for: 2 -> 2; matrix products, arithmetic and copies ran while one was open for 2% -> 4% of each run, Pallas kernels for 0% -> 0%
where the time goes in v1:
time: 475 us; the launch traced here: 472 us
  waiting for transfers between devices  370 us (78%)
  matrix products  33.8 us (7%)
  local copies, waits for them, and re-layouts  23.8 us (5%)
  blocking collectives  21.8 us (5%)
  between operations  14.1 us (3%)
  other arithmetic  8.08 us (2%)
    reduce_scatter x1, waiting for transfers between devices, per_device(): lax.psum_scatter(terms.astype(jnp.bfloat16), 'samp', scatter_dimension=0,...  272 us
    all_gather x1, waiting for transfers between devices, per_device(): lax.all_gather(design, 'feat', axis=1, tiled=True)  97.5 us
    dot_general x1, matrix products, per_device(): lax.dot_general(lax.all_gather(design, 'feat', axis=1, tiled=True), weigh...  32.4 us
    gather x1, local copies, waits for them, and re-layouts, per_device(): beta = coef_all[active]  14.5 us
    psum x1, blocking collectives, per_device(): margin = lax.psum(partial_margin, 'feat')  13.7 us
  transfers between devices with their start and end apart: 2, of which 2 were waited for; matrix products, arithmetic and copies ran while one was open for 4% of the time, Pallas kernels for 0%

profile of v1, /device:TPU:28, one launch (start us, length us, event | category | flops | bytes accessed | tf_op | source)
XLA Modules:
  0.0 471.8 jit_solution(10799739271853022834)
XLA Ops:
  7.2 0.0 copy-start
  7.2 0.0 copy-start.1
  7.2 0.0 all-gather.2.cloned.1.call-start
  7.2 0.7 all-gather.2.cloned.1.call-update
  7.9 0.0 reduce-scatter.2.cloned.1.call-start
  8.0 0.9 fusion.1
  8.8 14.5 %gather_fusion = f32[1024]{0:T(1024)S(1)} fusion(f32[1048576]{0:T(1024)} %param.7, s32[1024]{0:T(1024)S(1)} %fusion.1), kind=kCustom, calls=%fused_computation | custom fusion | bytes 12288 | tf_op jit(solution)/shard_map/gather | solution.py:11
  23.3 0.0 copy-done
  23.3 0.9 convolution_reduce_fusion
  24.3 13.7 %psum.14 = f32[1536]{0:T(1024)S(1)} all-reduce(f32[1536]{0:T(1024)S(1)} %convolution_reduce_fusion), channel_id=1, replica_groups=mesh['samp'=4,'feat'=8] {'feat'}, use_global_device_ids=true, to_apply=%region_0.0 | all-reduce | flops 1536 | bytes 12288 | tf_op jit(solution)/shard_map/psum | solution.py:13
  38.0 0.0 copy-done.1
  38.0 97.5 %all-gather.2.cloned.1.call-done = bf16[1536,8192]{1,0:T(8,128)(2,1)} async-done(((bf16[1536,1024]{1,0:T(8,128)(2,1)}), bf16[1536,8192]{1,0:T(8,128)(2,1)}) %all-gather.2.cloned.1.call-update) | async-done | bytes 25165840 | tf_op jit(solution)/shard_map/all_gather | solution.py:22
  135.6 32.4 %convert_bitcast_fusion = bf16[8192,1024]{0,1:T(8,128)(2,1)} fusion(bf16[1536,8192]{1,0:T(8,128)(2,1)} %all-gather.2.cloned.1.call-done, bf16[1536,1024]{1,0:T(8,128)(2,1)S(1)} %copy-done, f32[1536]{0:T(1024)S(1)} %get-tuple-element.7), kind=kOutput, calls=%fused_computation.1 | convolution fusion | flops 25782910976 | bytes 45094912 | tf_op jit(solution)/shard_map/dot_general | solution.py:21
  167.9 0.0 copy-start.2
  167.9 0.0 reduce-scatter.2.cloned.1.call-update
  168.0 0.5 fusion.2
  168.5 8.1 %psum.15 = f32[1024]{0:T(1024)S(1)} all-reduce(f32[1024]{0:T(1024)S(1)} %bitcast.8), channel_id=1, replica_groups=mesh['samp'=4,'feat'=8] {'samp'}, use_global_device_ids=true, to_apply=%region_2.0 | all-reduce | flops 1024 | bytes 8192 | tf_op jit(solution)/shard_map/psum | solution.py:20
  176.6 0.0 copy-done.2
  176.6 0.6 multiply_add_fusion
  177.2 272.0 %reduce-scatter.2.cloned.1.call-done = bf16[2048,1024]{0,1:T(8,128)(2,1)} async-done(((bf16[8192,1024]{0,1:T(8,128)(2,1)}), bf16[2048,1024]{0,1:T(8,128)(2,1)}) %reduce-scatter.2.cloned.1.call-update) | async-done | bytes 4194320 | tf_op jit(solution)/shard_map/reduce_scatter | solution.py:27
  449.1 6.6 %convert_multiply_fusion = f32[2048,1024]{0,1:T(8,128)} fusion(bf16[2048,1024]{0,1:T(8,128)(2,1)} %reduce-scatter.2.cloned.1.call-done), kind=kLoop, calls=%fused_computation.2 | loop fusion | flops 4194304 | bytes 12582912 | tf_op jit(solution)/shard_map/mul | solution.py:27
  455.8 9.2 %copy.8 = f32[2048,1024]{1,0:T(8,128)} copy(f32[2048,1024]{0,1:T(8,128)} %convert_multiply_fusion) | data formatting | bytes 16777216
  (4 shorter events, 0.0 us)
Async XLA Ops:
  7.2 16.2 %copy-start = (bf16[1536,1024]{1,0:T(8,128)(2,1)S(1)}, bf16[1536,1024]{1,0:T(8,128)(2,1)}, u32[]{:S(2)}) copy-start(bf16[1536,1024]{1,0:T(8,128)(2,1)} %param.5) | copy-start | bytes 9437188
  7.2 30.8 %copy-start.1 = (s32[1536]{0:T(1024)S(1)}, s32[1536]{0:T(1024)}, u32[]{:S(2)}) copy-start(s32[1536]{0:T(1024)} %param.6) | copy-start | bytes 18436
  7.2 128.4 %all-gather.2.cloned.1.call-start = ((), (), s32[]{:S(2)}) async-start(), calls=%async_computation.1 | async-start | bytes 28311552 | tf_op jit(solution)/shard_map/all_gather | solution.py:22
  7.9 441.2 %reduce-scatter.2.cloned.1.call-start = ((), (), s32[]{:S(2)}) async-start(), calls=%async_computation.2 | async-start | bytes 20971520 | tf_op jit(solution)/shard_map/reduce_scatter | solution.py:27
  167.9 8.6 %copy-start.2 = (f32[1024]{0:T(1024)S(1)}, f32[1024]{0:T(1024)}, u32[]{:S(2)}) copy-start(f32[1024]{0:T(1024)} %param.9) | copy-start | bytes 12292
Sparse Core Ops, SparseCore 0:
  9.9 125.5 all-gather.1
  168.1 281.0 reduce-scatter.1

commit v2 on v1

v2 whole, which is shorter than its diff:
```python
import functools

import jax
import jax.numpy as jnp
from jax import lax
from jax.experimental import pallas as pl
from jax.experimental.pallas import tpu as pltpu
from jax.sharding import PartitionSpec as P

MESH = pl.DeviceIdType.MESH


def kernel(nz, nc, nch, x_ref, w_ref, r_ref, acc_ref, grad_ref, col, row, wt,
           own_sem, z_send, z_recv, ring_send, ring_recv, sib_send, sib_recv, loc_sem):
    s = lax.axis_index("samp")
    f = lax.axis_index("feat")
    c, k = f // 2, f % 2

    def flip(p):
        return jnp.where(p < nc // 2, p, 3 * nc // 2 - 1 - p)

    pos = flip(c)
    d = lax.rem(pos - flip(s) + nc, nc)
    nxt = (s, 2 * flip(lax.rem(pos + 1, nc)) + k)
    prv = (s, 2 * flip(lax.rem(pos + nc - 1, nc)) + k)
    sib = (s, 2 * c + 1 - k)
    width = wt.shape[1]
    tile = min(256, width)

    own = pltpu.make_async_copy(x_ref, col.at[s], own_sem)
    own.start()
    acc_ref[...] = jnp.zeros_like(acc_ref)
    grad_ref[...] = jnp.zeros_like(grad_ref)

    barrier = pltpu.get_barrier_semaphore()
    for dev in (nxt, prv, sib):
        pl.semaphore_signal(barrier, inc=1, device_id=dev, device_id_type=MESH)

    @pl.when(s > 0)
    def _():
        pl.semaphore_signal(barrier, inc=1, device_id=(s - 1, f), device_id_type=MESH)

    @pl.when(s < nz - 1)
    def _():
        pl.semaphore_signal(barrier, inc=1, device_id=(s + 1, f), device_id_type=MESH)

    pl.semaphore_wait(barrier, 3 + (s > 0).astype(jnp.int32) + (s < nz - 1).astype(jnp.int32))
    own.wait()

    def z_copy(o, i, way):
        return pltpu.make_async_remote_copy(
            col.at[o, i], col.at[o, i], z_send.at[o, i, way], z_recv.at[o, i],
            device_id=(s + 1 - 2 * way, f), device_id_type=MESH)

    def ring_copy(src, o, i, dev):
        return pltpu.make_async_remote_copy(
            src.at[o, i], row.at[k, o, i], ring_send.at[o, i], ring_recv.at[o, i],
            device_id=dev, device_id_type=MESH)

    def sib_copy(src, o, i):
        return pltpu.make_async_remote_copy(
            src.at[o, i], row.at[k, o, i], sib_send.at[o, i], sib_recv.at[o, i],
            device_id=sib, device_id_type=MESH)

    def sib_wait(o, i):
        pltpu.make_async_remote_copy(
            row.at[1 - k, o, i], row.at[1 - k, o, i], sib_send.at[o, i], sib_recv.at[o, i],
            device_id=sib, device_id_type=MESH).wait_recv()

    def loc_copy(o, i):
        return pltpu.make_async_copy(col.at[o, i], row.at[k, o, i], loc_sem.at[o, i])

    def send_own(i):
        @pl.when(s < nz - 1)
        def _():
            z_copy(s, i, 0).start()

        @pl.when(s > 0)
        def _():
            z_copy(s, i, 1).start()

    def is_cw(o, i):
        return lax.rem(i + (o > s).astype(jnp.int32), 2) == 0

    def spread(o, i):
        @pl.when(d == 0)
        def _():
            cw = is_cw(o, i)

            @pl.when(cw)
            def _():
                ring_copy(col, o, i, nxt).start()

            @pl.when(jnp.logical_not(cw))
            def _():
                ring_copy(col, o, i, prv).start()

            sib_copy(col, o, i).start()
            loc_copy(o, i).start()

    def passing(o, i, cw):
        @pl.when(is_cw(o, i) == cw)
        def _():
            mine = row.at[k]
            ring_copy(mine, o, i, nxt).wait_recv()
            if cw:
                @pl.when(d < nc - 1)
                def _():
                    ring_copy(mine, o, i, nxt).start()
            else:
                @pl.when(d > 1)
                def _():
                    ring_copy(mine, o, i, prv).start()
            sib_copy(mine, o, i).start()

    def compute(o, i):
        sib_wait(o, i)

        @pl.when(d == 0)
        def _():
            loc_copy(o, i).wait()

        block = col[o, i]
        wt[...] = (block.astype(jnp.float32) * w_ref[o, i]).astype(jnp.bfloat16)
        grad_ref[...] += jnp.dot(r_ref[o, i], block, preferred_element_type=jnp.float32)
        for kk in range(2):
            @pl.loop(0, width // tile)
            def _(m):
                at = pl.multiple_of(m * tile, tile)
                lhs = row[kk, o, i, :, pl.ds(at, tile)]
                acc_ref[pl.ds(kk * width + at, tile), :] += lax.dot_general(
                    lhs, wt[...], (((0,), (0,)), ((), ())), preferred_element_type=jnp.float32)

    steps = (nz - 1) * nch

    def events(e, fn):
        @pl.when(jnp.logical_and(e >= 0, e < steps))
        def _():
            j = e // nch + 1
            i = e % nch

            @pl.when(j == 1)
            def _():
                fn(s, i)

            @pl.when(s - j >= 0)
            def _():
                fn(s - j, i)

            @pl.when(s + j < nz)
            def _():
                fn(s + j, i)

    def arrive(o, i):
        @pl.when(o != s)
        def _():
            z_copy(o, i, 0).wait_recv()

            @pl.when(jnp.logical_and(o < s, s < nz - 1))
            def _():
                z_copy(o, i, 0).start()

            @pl.when(jnp.logical_and(o > s, s > 0))
            def _():
                z_copy(o, i, 1).start()
        spread(o, i)

    send_own(0)

    @pl.loop(0, steps + nc)
    def _(t):
        @pl.when(t + 1 < nch)
        def _():
            send_own(t + 1)
        events(t, arrive)

        @pl.when(d > 0)
        def _():
            events(t - d, lambda o, i: passing(o, i, True))
            events(t - (nc - d), lambda o, i: passing(o, i, False))
        events(t - nc, compute)

    @pl.loop(0, nz * nch)
    def _(q):
        o = q // nch
        i = q % nch

        @pl.when(jnp.logical_and(o <= s, s < nz - 1))
        def _():
            z_copy(o, i, 0).wait_send()

        @pl.when(jnp.logical_and(o >= s, s > 0))
        def _():
            z_copy(o, i, 1).wait_send()

        sib_copy(row.at[k], o, i).wait_send()
        cw = is_cw(o, i)

        @pl.when(jnp.logical_or(jnp.logical_and(cw, d < nc - 1),
                                jnp.logical_and(jnp.logical_not(cw), d != 1)))
        def _():
            ring_copy(row.at[k], o, i, nxt).wait_send()


def per_device(nz, nf, design, labels, coef_all, active, penalty):
    rows, width = design.shape
    nc = nf // 2
    nch = 6
    ch = rows // nch
    scale = 1.0 / jnp.sqrt(jnp.float32(rows * nz))
    beta = coef_all[active]
    partial_margin = jnp.dot(design, beta.astype(jnp.bfloat16), preferred_element_type=jnp.float32)
    margin = lax.psum(partial_margin, "feat")
    prob = 1.0 / (1.0 + jnp.exp(-margin))
    weight = prob * (1.0 - prob)
    resid = prob - labels.astype(jnp.float32)
    both = lax.all_gather(jnp.stack([weight, resid]), "samp", axis=0)
    w4 = both[:, 0].reshape(nz, nch, ch, 1)
    r4 = jnp.broadcast_to(both[:, 1].astype(jnp.bfloat16).reshape(nz, nch, 1, ch), (nz, nch, 16, ch))
    vmem = pl.BlockSpec(memory_space=pltpu.VMEM)
    dma = pltpu.SemaphoreType.DMA
    terms, grad = pl.pallas_call(
        functools.partial(kernel, nz, nc, nch),
        out_shape=(jax.ShapeDtypeStruct((2 * width, width), jnp.float32),
                   jax.ShapeDtypeStruct((16, width), jnp.float32)),
        in_specs=[pl.BlockSpec(memory_space=pl.ANY), vmem, vmem],
        out_specs=(vmem, vmem),
        scratch_shapes=[
            pltpu.VMEM((nz, nch, ch, width), jnp.bfloat16),
            pltpu.VMEM((2, nz, nch, ch, width), jnp.bfloat16),
            pltpu.VMEM((ch, width), jnp.bfloat16),
            dma,
            dma((nz, nch, 2)),
            dma((nz, nch)),
            dma((nz, nch)),
            dma((nz, nch)),
            dma((nz, nch)),
            dma((nz, nch)),
            dma((nz, nch)),
        ],
        compiler_params=pltpu.CompilerParams(
            collective_id=0, has_side_effects=True, vmem_limit_bytes=60 * 1024 * 1024),
        cost_estimate=pl.CostEstimate(
            flops=4 * nz * rows * width * width, bytes_accessed=2 * rows * width + 8 * width * width,
            transcendentals=0),
    )(design.reshape(nch, ch, width), w4, r4)
    return terms * scale, grad[0] * scale + penalty * beta


def solution(mesh):
    in_specs = (P("samp", "feat"), P("samp"), P(), P("feat"), P("feat"))
    out_specs = (P("samp", "feat"), P("feat"))
    return jax.shard_map(
        functools.partial(per_device, mesh.shape["samp"], mesh.shape["feat"]),
        mesh=mesh, in_specs=in_specs, out_specs=out_specs, check_vma=False
    )
```

time: 475 us -> 328 us (0.69)
  waiting for transfers between devices: 370 us -> 0 us
  Pallas kernels: 0 us -> 269 us
  matrix products: 33.8 us -> 0.93 us
  between operations: 14.1 us -> 0.74 us
  local copies, waits for them, and re-layouts: 23.8 us -> 19 us
    reduce_scatter x1 -> x0, waiting for transfers between devices: 272 us -> none  [per_device(): lax.psum_scatter(terms.astype(jnp.bfloat16), 'samp', scatter_dimension=0,...]
    pallas_call x0 -> x1, Pallas kernels: none -> 269 us  [per_device(): pl.pallas_call(functools.partial(kernel, nz, nc, nch), out_shape=(jax.Sha...]
    all_gather x1 -> x0, waiting for transfers between devices: 97.5 us -> none  [per_device(): lax.all_gather(design, 'feat', axis=1, tiled=True)]
    dot_general x2 -> x0, matrix products: 32.9 us -> none  [the longest x1 32.4 us: per_device(): lax.dot_general(lax.all_gather(design, 'feat', axis=1, tiled=True), weigh...]
    all_gather x0 -> x1, blocking collectives: none -> 13.1 us  [per_device(): both = lax.all_gather(jnp.stack([weight, resid]), 'samp', axis=0)]
    unnamed x7 -> x6, local copies, waits for them, and re-layouts: 9.25 us -> 0.01 us
    psum x1 -> x0, blocking collectives: 8.08 us -> none  [per_device(): gradient = lax.psum(grad_part, 'samp') * scale + penalty * beta]
    mul x1 -> x3, other arithmetic: 6.61 us -> 9.55 us  [the longest x2 9.54 us: per_device(): return (terms * scale, grad[0] * scale + penalty * beta)]
  transfers between devices with their start and end apart: 2 -> 0, of which waited for: 2 -> 0; matrix products, arithmetic and copies ran while one was open for 4% -> 0% of each run, Pallas kernels for 0% -> 0%
where the time goes in v2:
time: 328 us; the launch traced here: 327 us
  Pallas kernels  269 us (82%)
  blocking collectives  26 us (8%)
  local copies, waits for them, and re-layouts  19 us (6%)
  other arithmetic  11 us (3%)
    pallas_call x1, Pallas kernels, per_device(): pl.pallas_call(functools.partial(kernel, nz, nc, nch), out_shape=(jax.Sha...  269 us
    gather x1, local copies, waits for them, and re-layouts, per_device(): beta = coef_all[active]  13.4 us
    all_gather x1, blocking collectives, per_device(): both = lax.all_gather(jnp.stack([weight, resid]), 'samp', axis=0)  13.1 us
    psum x1, blocking collectives, per_device(): margin = lax.psum(partial_margin, 'feat')  13 us
    mul x2, other arithmetic, per_device(): return (terms * scale, grad[0] * scale + penalty * beta)  9.54 us

profile of v2, /device:TPU:28, one launch (start us, length us, event | category | flops | bytes accessed | tf_op | source)
XLA Modules:
  0.0 326.9 jit_solution(6391339976508641751)
XLA Ops:
  0.6 0.0 copy-start
  0.6 0.0 copy-start.1
  0.7 0.8 fusion.1
  1.5 13.4 %gather_fusion = f32[1024]{0:T(1024)S(1)} fusion(f32[1048576]{0:T(1024)} %param.7, s32[1024]{0:T(1024)S(1)} %fusion.1), kind=kCustom, calls=%fused_computation | custom fusion | bytes 12288 | tf_op jit(solution)/shard_map/gather | solution.py:211
  14.9 0.0 copy-done
  14.9 0.9 convolution_reduce_fusion
  15.9 13.0 %psum.7 = f32[1536]{0:T(1024)S(1)} all-reduce(f32[1536]{0:T(1024)S(1)} %convolution_reduce_fusion), channel_id=1, replica_groups=mesh['samp'=4,'feat'=8] {'feat'}, use_global_device_ids=true, to_apply=%region_0.0 | all-reduce | flops 1536 | bytes 12288 | tf_op jit(solution)/shard_map/psum | solution.py:213
  28.9 0.0 copy-done.1
  28.9 13.1 %all-gather.1 = f32[4,2,1536]{2,1,0:T(2,128)S(1)} all-gather(f32[1,2,1536]{2,1,0:T(2,128)S(1)} %maximum_bitcast_fusion), channel_id=2, replica_groups=mesh['samp'=4,'feat'=8] {'samp'}, dimensions={0}, use_global_device_ids=true | all-gather | bytes 61440 | tf_op jit(solution)/shard_map/all_gather | solution.py:217
  42.0 0.1 slice_reduce_fusion
  42.1 4.7 %reshape_squeeze.4.w_ref = f32[4,6,256,1]{3,2,1,0:T(8,128)} reshape(f32[4,1536]{1,0:T(4,128)S(1)} %slice_reduce_fusion) | data formatting | bytes 49152 | tf_op jit(solution)/shard_map/reshape;squeeze | solution.py:218
  46.8 0.1 fusion
  46.9 0.7 broadcast_in_dim.9.r_ref
  47.6 0.0 copy-start.2
  47.6 269.2 %shard_map.68 = (f32[2048,1024]{1,0:T(8,128)}, f32[16,1024]{1,0:T(8,128)}) custom-call(bf16[6,256,1024]{2,1,0:T(8,128)(2,1)} %bitcast.6, f32[4,6,256,1]{3,2,1,0:T(8,128)} %reshape_squeeze.4.w_ref, bf16[4,6,16,256]{3,2,1,0:T(8,128)(2,1)} %broadcast_in_dim.9.r_ref), custom_call_target="tpu_custom_call" | custom-call | flops 25769803776 | bytes 11534336 | tf_op jit(solution)/shard_map/pallas_call | solution.py:222
  316.8 0.8 slice_multiply_fusion
  317.6 0.0 copy-done.2
  317.6 0.6 multiply_add_fusion
  318.2 8.8 %broadcast_multiply_fusion = f32[2048,1024]{1,0:T(8,128)} fusion(f32[2048,1024]{1,0:T(8,128)} %get-tuple-element.4), kind=kLoop, calls=%fused_computation.1 | loop fusion | flops 2097152 | bytes 16777216 | tf_op jit(solution)/shard_map/mul | solution.py:247
  (7 shorter events, 0.1 us)
Async XLA Ops:
  0.6 14.3 %copy-start = (bf16[1536,1024]{1,0:T(8,128)(2,1)S(1)}, bf16[1536,1024]{1,0:T(8,128)(2,1)}, u32[]{:S(2)}) copy-start(bf16[1536,1024]{1,0:T(8,128)(2,1)} %param.5) | copy-start | bytes 9437188
  0.6 28.2 %copy-start.1 = (s32[1536]{0:T(1024)S(1)}, s32[1536]{0:T(1024)}, u32[]{:S(2)}) copy-start(s32[1536]{0:T(1024)} %param.6) | copy-start | bytes 18436
  47.6 270.0 %copy-start.2 = (f32[1024]{0:T(1024)S(1)}, f32[1024]{0:T(1024)}, u32[]{:S(2)}) copy-start(f32[1024]{0:T(1024)} %param.9) | copy-start | bytes 12292

commit v3 on v2

--- a/solution.py
+++ b/solution.py
@@ -205,7 +205,7 @@
 def per_device(nz, nf, design, labels, coef_all, active, penalty):
     rows, width = design.shape
     nc = nf // 2
-    nch = 6
+    nch = 12
     ch = rows // nch
     scale = 1.0 / jnp.sqrt(jnp.float32(rows * nz))
     beta = coef_all[active]

time: 328 us -> 342 us (1.043)
  Pallas kernels: 269 us -> 284 us
    pallas_call x1, Pallas kernels: 269 us -> 284 us  [per_device(): pl.pallas_call(functools.partial(kernel, nz, nc, nch), out_shape=(jax.Sha...]
where the time goes in v3:
time: 342 us
  Pallas kernels  284 us (83%)
  blocking collectives  26 us (8%)
  local copies, waits for them, and re-layouts  19 us (6%)
  other arithmetic  11 us (3%)
    pallas_call x1, Pallas kernels, per_device(): pl.pallas_call(functools.partial(kernel, nz, nc, nch), out_shape=(jax.Sha...  284 us
    gather x1, local copies, waits for them, and re-layouts, per_device(): beta = coef_all[active]  13.4 us
    all_gather x1, blocking collectives, per_device(): both = lax.all_gather(jnp.stack([weight, resid]), 'samp', axis=0)  13.1 us
    psum x1, blocking collectives, per_device(): margin = lax.psum(partial_margin, 'feat')  13 us
    mul x2, other arithmetic, per_device(): return (terms * scale, grad[0] * scale + penalty * beta)  9.54 us

profile of v3, /device:TPU:28, one launch (start us, length us, event | category | flops | bytes accessed | tf_op | source)
XLA Modules:
  0.0 341.6 jit_solution(13762620427720059651)
XLA Ops:
  0.6 0.0 copy-start
  0.6 0.0 copy-start.1
  0.7 0.8 fusion.1
  1.5 13.4 %gather_fusion = f32[1024]{0:T(1024)S(1)} fusion(f32[1048576]{0:T(1024)} %param.7, s32[1024]{0:T(1024)S(1)} %fusion.1), kind=kCustom, calls=%fused_computation | custom fusion | bytes 12288 | tf_op jit(solution)/shard_map/gather | solution.py:211
  14.9 0.0 copy-done
  14.9 0.9 convolution_reduce_fusion
  15.9 13.0 %psum.7 = f32[1536]{0:T(1024)S(1)} all-reduce(f32[1536]{0:T(1024)S(1)} %convolution_reduce_fusion), channel_id=1, replica_groups=mesh['samp'=4,'feat'=8] {'feat'}, use_global_device_ids=true, to_apply=%region_0.0 | all-reduce | flops 1536 | bytes 12288 | tf_op jit(solution)/shard_map/psum | solution.py:213
  28.9 0.0 copy-done.1
  28.9 13.1 %all-gather.1 = f32[4,2,1536]{2,1,0:T(2,128)S(1)} all-gather(f32[1,2,1536]{2,1,0:T(2,128)S(1)} %maximum_bitcast_fusion), channel_id=2, replica_groups=mesh['samp'=4,'feat'=8] {'samp'}, dimensions={0}, use_global_device_ids=true | all-gather | bytes 61440 | tf_op jit(solution)/shard_map/all_gather | solution.py:217
  42.0 0.1 slice_reduce_fusion
  42.1 4.7 %reshape_squeeze.4.w_ref = f32[4,12,128,1]{3,2,1,0:T(8,128)} reshape(f32[4,1536]{1,0:T(4,128)S(1)} %slice_reduce_fusion) | data formatting | bytes 49152 | tf_op jit(solution)/shard_map/reshape;squeeze | solution.py:218
  46.8 0.1 fusion
  46.9 0.7 broadcast_in_dim.9.r_ref
  47.6 0.0 copy-start.2
  47.6 283.8 %shard_map.68 = (f32[2048,1024]{1,0:T(8,128)}, f32[16,1024]{1,0:T(8,128)}) custom-call(bf16[12,128,1024]{2,1,0:T(8,128)(2,1)} %bitcast.6, f32[4,12,128,1]{3,2,1,0:T(8,128)} %reshape_squeeze.4.w_ref, bf16[4,12,16,128]{3,2,1,0:T(8,128)(2,1)} %broadcast_in_dim.9.r_ref), custom_call_target="tpu_custom_call" | custom-call | flops 25769803776 | bytes 11534336 | tf_op jit(solution)/shard_map/pallas_call | solution.py:222
  331.4 0.8 slice_multiply_fusion
  332.2 0.0 copy-done.2
  332.2 0.6 multiply_add_fusion
  332.8 8.8 %broadcast_multiply_fusion = f32[2048,1024]{1,0:T(8,128)} fusion(f32[2048,1024]{1,0:T(8,128)} %get-tuple-element.4), kind=kLoop, calls=%fused_computation.1 | loop fusion | flops 2097152 | bytes 16777216 | tf_op jit(solution)/shard_map/mul | solution.py:247
  (7 shorter events, 0.1 us)
Async XLA Ops:
  0.6 14.3 %copy-start = (bf16[1536,1024]{1,0:T(8,128)(2,1)S(1)}, bf16[1536,1024]{1,0:T(8,128)(2,1)}, u32[]{:S(2)}) copy-start(bf16[1536,1024]{1,0:T(8,128)(2,1)} %param.5) | copy-start | bytes 9437188
  0.6 28.2 %copy-start.1 = (s32[1536]{0:T(1024)S(1)}, s32[1536]{0:T(1024)}, u32[]{:S(2)}) copy-start(s32[1536]{0:T(1024)} %param.6) | copy-start | bytes 18436
  47.6 284.6 %copy-start.2 = (f32[1024]{0:T(1024)S(1)}, f32[1024]{0:T(1024)}, u32[]{:S(2)}) copy-start(f32[1024]{0:T(1024)} %param.9) | copy-start | bytes 12292

commit v4 on v3

--- a/solution.py
+++ b/solution.py
@@ -24,7 +24,7 @@
     nxt = (s, 2 * flip(lax.rem(pos + 1, nc)) + k)
     prv = (s, 2 * flip(lax.rem(pos + nc - 1, nc)) + k)
     sib = (s, 2 * c + 1 - k)
-    width = wt.shape[1]
+    depth, width = wt.shape
     tile = min(256, width)
 
     own = pltpu.make_async_copy(x_ref, col.at[s], own_sem)
@@ -120,16 +120,19 @@
         def _():
             loc_copy(o, i).wait()
 
-        block = col[o, i]
-        wt[...] = (block.astype(jnp.float32) * w_ref[o, i]).astype(jnp.bfloat16)
-        grad_ref[...] += jnp.dot(r_ref[o, i], block, preferred_element_type=jnp.float32)
-        for kk in range(2):
-            @pl.loop(0, width // tile)
-            def _(m):
-                at = pl.multiple_of(m * tile, tile)
-                lhs = row[kk, o, i, :, pl.ds(at, tile)]
-                acc_ref[pl.ds(kk * width + at, tile), :] += lax.dot_general(
-                    lhs, wt[...], (((0,), (0,)), ((), ())), preferred_element_type=jnp.float32)
+        @pl.when(i % 2 == 1)
+        def _():
+            pair = pl.ds(i - 1, 2)
+            block = col[o, pair].reshape(depth, width)
+            wt[...] = (block.astype(jnp.float32) * w_ref[o, i // 2]).astype(jnp.bfloat16)
+            grad_ref[...] += jnp.dot(r_ref[o, i // 2], block, preferred_element_type=jnp.float32)
+            for kk in range(2):
+                @pl.loop(0, width // tile)
+                def _(m):
+                    at = pl.multiple_of(m * tile, tile)
+                    lhs = row[kk, o, pair, :, pl.ds(at, tile)].reshape(depth, tile)
+                    acc_ref[pl.ds(kk * width + at, tile), :] += lax.dot_general(
+                        lhs, wt[...], (((0,), (0,)), ((), ())), preferred_element_type=jnp.float32)
 
     steps = (nz - 1) * nch
 
@@ -166,12 +169,13 @@
         spread(o, i)
 
     send_own(0)
+    send_own(1)
 
     @pl.loop(0, steps + nc)
     def _(t):
-        @pl.when(t + 1 < nch)
-        def _():
-            send_own(t + 1)
+        @pl.when(t + 2 < nch)
+        def _():
+            send_own(t + 2)
         events(t, arrive)
 
         @pl.when(d > 0)
@@ -215,8 +219,8 @@
     weight = prob * (1.0 - prob)
     resid = prob - labels.astype(jnp.float32)
     both = lax.all_gather(jnp.stack([weight, resid]), "samp", axis=0)
-    w4 = both[:, 0].reshape(nz, nch, ch, 1)
-    r4 = jnp.broadcast_to(both[:, 1].astype(jnp.bfloat16).reshape(nz, nch, 1, ch), (nz, nch, 16, ch))
+    w4 = both[:, 0].reshape(nz, nch // 2, 2 * ch, 1)
+    r4 = jnp.broadcast_to(both[:, 1].astype(jnp.bfloat16).reshape(nz, nch // 2, 1, 2 * ch), (nz, nch // 2, 16, 2 * ch))
     vmem = pl.BlockSpec(memory_space=pltpu.VMEM)
     dma = pltpu.SemaphoreType.DMA
     terms, grad = pl.pallas_call(
@@ -228,7 +232,7 @@
         scratch_shapes=[
             pltpu.VMEM((nz, nch, ch, width), jnp.bfloat16),
             pltpu.VMEM((2, nz, nch, ch, width), jnp.bfloat16),
-            pltpu.VMEM((ch, width), jnp.bfloat16),
+            pltpu.VMEM((2 * ch, width), jnp.bfloat16),
             dma,
             dma((nz, nch, 2)),
             dma((nz, nch)),

time: 342 us -> 345 us (level)
  no operation moved by 1% of the time
where the time goes in v4:
time: 345 us; the launch traced here: 344 us
  Pallas kernels  286 us (83%)
  blocking collectives  26 us (8%)
  local copies, waits for them, and re-layouts  19 us (6%)
  other arithmetic  11 us (3%)
    pallas_call x1, Pallas kernels, per_device(): pl.pallas_call(functools.partial(kernel, nz, nc, nch), out_shape=(jax.Sha...  286 us
    gather x1, local copies, waits for them, and re-layouts, per_device(): beta = coef_all[active]  13.4 us
    all_gather x1, blocking collectives, per_device(): both = lax.all_gather(jnp.stack([weight, resid]), 'samp', axis=0)  13.1 us
    psum x1, blocking collectives, per_device(): margin = lax.psum(partial_margin, 'feat')  13 us
    mul x2, other arithmetic, per_device(): return (terms * scale, grad[0] * scale + penalty * beta)  9.54 us

profile of v4, /device:TPU:28, one launch (start us, length us, event | category | flops | bytes accessed | tf_op | source)
XLA Modules:
  0.0 343.9 jit_solution(17065805936537642300)
XLA Ops:
  0.6 0.0 copy-start
  0.6 0.0 copy-start.1
  0.7 0.8 fusion.1
  1.5 13.4 %gather_fusion = f32[1024]{0:T(1024)S(1)} fusion(f32[1048576]{0:T(1024)} %param.7, s32[1024]{0:T(1024)S(1)} %fusion.1), kind=kCustom, calls=%fused_computation | custom fusion | bytes 12288 | tf_op jit(solution)/shard_map/gather | solution.py:215
  14.9 0.0 copy-done
  14.9 0.9 convolution_reduce_fusion
  15.9 13.0 %psum.7 = f32[1536]{0:T(1024)S(1)} all-reduce(f32[1536]{0:T(1024)S(1)} %convolution_reduce_fusion), channel_id=1, replica_groups=mesh['samp'=4,'feat'=8] {'feat'}, use_global_device_ids=true, to_apply=%region_0.0 | all-reduce | flops 1536 | bytes 12288 | tf_op jit(solution)/shard_map/psum | solution.py:217
  28.9 0.0 copy-done.1
  28.9 13.1 %all-gather.1 = f32[4,2,1536]{2,1,0:T(2,128)S(1)} all-gather(f32[1,2,1536]{2,1,0:T(2,128)S(1)} %maximum_bitcast_fusion), channel_id=2, replica_groups=mesh['samp'=4,'feat'=8] {'samp'}, dimensions={0}, use_global_device_ids=true | all-gather | bytes 61440 | tf_op jit(solution)/shard_map/all_gather | solution.py:221
  42.0 0.1 slice_reduce_fusion
  42.1 4.7 %reshape_squeeze.4.w_ref = f32[4,6,256,1]{3,2,1,0:T(8,128)} reshape(f32[4,1536]{1,0:T(4,128)S(1)} %slice_reduce_fusion) | data formatting | bytes 49152 | tf_op jit(solution)/shard_map/reshape;squeeze | solution.py:222
  46.8 0.1 fusion
  46.9 0.7 broadcast_in_dim.9.r_ref
  47.6 0.0 copy-start.2
  47.6 286.1 %shard_map.68 = (f32[2048,1024]{1,0:T(8,128)}, f32[16,1024]{1,0:T(8,128)}) custom-call(bf16[12,128,1024]{2,1,0:T(8,128)(2,1)} %bitcast.6, f32[4,6,256,1]{3,2,1,0:T(8,128)} %reshape_squeeze.4.w_ref, bf16[4,6,16,256]{3,2,1,0:T(8,128)(2,1)} %broadcast_in_dim.9.r_ref), custom_call_target="tpu_custom_call" | custom-call | flops 25769803776 | bytes 11534336 | tf_op jit(solution)/shard_map/pallas_call | solution.py:226
  333.7 0.8 slice_multiply_fusion
  334.5 0.0 copy-done.2
  334.5 0.6 multiply_add_fusion
  335.1 8.8 %broadcast_multiply_fusion = f32[2048,1024]{1,0:T(8,128)} fusion(f32[2048,1024]{1,0:T(8,128)} %get-tuple-element.4), kind=kLoop, calls=%fused_computation.1 | loop fusion | flops 2097152 | bytes 16777216 | tf_op jit(solution)/shard_map/mul | solution.py:251
  (7 shorter events, 0.1 us)
Async XLA Ops:
  0.6 14.3 %copy-start = (bf16[1536,1024]{1,0:T(8,128)(2,1)S(1)}, bf16[1536,1024]{1,0:T(8,128)(2,1)}, u32[]{:S(2)}) copy-start(bf16[1536,1024]{1,0:T(8,128)(2,1)} %param.5) | copy-start | bytes 9437188
  0.6 28.2 %copy-start.1 = (s32[1536]{0:T(1024)S(1)}, s32[1536]{0:T(1024)}, u32[]{:S(2)}) copy-start(s32[1536]{0:T(1024)} %param.6) | copy-start | bytes 18436
  47.6 286.9 %copy-start.2 = (f32[1024]{0:T(1024)S(1)}, f32[1024]{0:T(1024)}, u32[]{:S(2)}) copy-start(f32[1024]{0:T(1024)} %param.9) | copy-start | bytes 12292

commit v5 on v3

--- a/solution.py
+++ b/solution.py
@@ -205,7 +205,7 @@
 def per_device(nz, nf, design, labels, coef_all, active, penalty):
     rows, width = design.shape
     nc = nf // 2
-    nch = 12
+    nch = 4
     ch = rows // nch
     scale = 1.0 / jnp.sqrt(jnp.float32(rows * nz))
     beta = coef_all[active]

time: 342 us -> 335 us (0.980)
  Pallas kernels: 284 us -> 277 us
    pallas_call x1, Pallas kernels: 284 us -> 277 us  [per_device(): pl.pallas_call(functools.partial(kernel, nz, nc, nch), out_shape=(jax.Sha...]
where the time goes in v5:
time: 335 us
  Pallas kernels  277 us (83%)
  blocking collectives  26 us (8%)
  local copies, waits for them, and re-layouts  19 us (6%)
  other arithmetic  11 us (3%)
    pallas_call x1, Pallas kernels, per_device(): pl.pallas_call(functools.partial(kernel, nz, nc, nch), out_shape=(jax.Sha...  277 us
    gather x1, local copies, waits for them, and re-layouts, per_device(): beta = coef_all[active]  13.4 us
    all_gather x1, blocking collectives, per_device(): both = lax.all_gather(jnp.stack([weight, resid]), 'samp', axis=0)  13.1 us
    psum x1, blocking collectives, per_device(): margin = lax.psum(partial_margin, 'feat')  13 us
    mul x2, other arithmetic, per_device(): return (terms * scale, grad[0] * scale + penalty * beta)  9.54 us

profile of v5, /device:TPU:28, one launch (start us, length us, event | category | flops | bytes accessed | tf_op | source)
XLA Modules:
  0.0 334.7 jit_solution(4237584186075730165)
XLA Ops:
  0.6 0.0 copy-start
  0.6 0.0 copy-start.1
  0.7 0.8 fusion.1
  1.5 13.4 %gather_fusion = f32[1024]{0:T(1024)S(1)} fusion(f32[1048576]{0:T(1024)} %param.7, s32[1024]{0:T(1024)S(1)} %fusion.1), kind=kCustom, calls=%fused_computation | custom fusion | bytes 12288 | tf_op jit(solution)/shard_map/gather | solution.py:211
  14.9 0.0 copy-done
  14.9 0.9 convolution_reduce_fusion
  15.9 13.0 %psum.7 = f32[1536]{0:T(1024)S(1)} all-reduce(f32[1536]{0:T(1024)S(1)} %convolution_reduce_fusion), channel_id=1, replica_groups=mesh['samp'=4,'feat'=8] {'feat'}, use_global_device_ids=true, to_apply=%region_0.0 | all-reduce | flops 1536 | bytes 12288 | tf_op jit(solution)/shard_map/psum | solution.py:213
  28.9 0.0 copy-done.1
  28.9 13.1 %all-gather.1 = f32[4,2,1536]{2,1,0:T(2,128)S(1)} all-gather(f32[1,2,1536]{2,1,0:T(2,128)S(1)} %maximum_bitcast_fusion), channel_id=2, replica_groups=mesh['samp'=4,'feat'=8] {'samp'}, dimensions={0}, use_global_device_ids=true | all-gather | bytes 61440 | tf_op jit(solution)/shard_map/all_gather | solution.py:217
  42.0 0.1 slice_reduce_fusion
  42.1 4.7 %reshape_squeeze.4.w_ref = f32[4,4,384,1]{3,2,1,0:T(8,128)} reshape(f32[4,1536]{1,0:T(4,128)S(1)} %slice_reduce_fusion) | data formatting | bytes 49152 | tf_op jit(solution)/shard_map/reshape;squeeze | solution.py:218
  46.8 0.1 fusion
  46.9 0.7 broadcast_in_dim.9.r_ref
  47.6 0.0 copy-start.2
  47.6 276.9 %shard_map.68 = (f32[2048,1024]{1,0:T(8,128)}, f32[16,1024]{1,0:T(8,128)}) custom-call(bf16[4,384,1024]{2,1,0:T(8,128)(2,1)} %bitcast.6, f32[4,4,384,1]{3,2,1,0:T(8,128)} %reshape_squeeze.4.w_ref, bf16[4,4,16,384]{3,2,1,0:T(8,128)(2,1)} %broadcast_in_dim.9.r_ref), custom_call_target="tpu_custom_call" | custom-call | flops 25769803776 | bytes 11534336 | tf_op jit(solution)/shard_map/pallas_call | solution.py:222
  324.6 0.8 slice_multiply_fusion
  325.3 0.0 copy-done.2
  325.3 0.6 multiply_add_fusion
  325.9 8.8 %broadcast_multiply_fusion = f32[2048,1024]{1,0:T(8,128)} fusion(f32[2048,1024]{1,0:T(8,128)} %get-tuple-element.4), kind=kLoop, calls=%fused_computation.1 | loop fusion | flops 2097152 | bytes 16777216 | tf_op jit(solution)/shard_map/mul | solution.py:247
  (7 shorter events, 0.1 us)
Async XLA Ops:
  0.6 14.3 %copy-start = (bf16[1536,1024]{1,0:T(8,128)(2,1)S(1)}, bf16[1536,1024]{1,0:T(8,128)(2,1)}, u32[]{:S(2)}) copy-start(bf16[1536,1024]{1,0:T(8,128)(2,1)} %param.5) | copy-start | bytes 9437188
  0.6 28.2 %copy-start.1 = (s32[1536]{0:T(1024)S(1)}, s32[1536]{0:T(1024)}, u32[]{:S(2)}) copy-start(s32[1536]{0:T(1024)} %param.6) | copy-start | bytes 18436
  47.6 277.7 %copy-start.2 = (f32[1024]{0:T(1024)S(1)}, f32[1024]{0:T(1024)}, u32[]{:S(2)}) copy-start(f32[1024]{0:T(1024)} %param.9) | copy-start | bytes 12292
